TPU v7x, 32 devices: a whole 2x2x4 slice. The times are simulated.
32 devices in a mesh: row: 4 (over y, x), col: 8 (over z, core).
Axes of the slice: x: 2, y: 2, z: 4, core: 2. Of those that a mesh axis runs over, the one named last changes fastest.
Arguments:
- multiplier: float32 [512, 20480], P(('row', 'col')), may hold values from -6 to 6
- cycle_tiles: float32 [20480, 512], P('row', 'col'), may hold values from -0.0625 to 0.0625
Outputs:
- symmetric: float32 [512, 512], P(('row', 'col'))
All inputs are finite; a program needn't handle non-finite values.
Results may differ from a plain program's by a relative error of at most 0.00007.
Values sent between devices are 32-bit elements; how exact they have to be, the bound alone decides.
A program may use at most 64 MiB of HBM per device.

v0:
```python
import jax
import jax.numpy as jnp
from jax import lax
from jax.sharding import PartitionSpec as P

O = 40
V = 512
OW = 1


def on_device(multiplier, cycle_tiles):
    rows_loc, full_width = multiplier.shape
    row_count = lax.axis_size("row")
    col_count = lax.axis_size("col")
    devices = row_count * col_count
    block_width = full_width // devices
    out_block = cycle_tiles.shape[1] // row_count
    virt_dev = rows_loc // OW
    all_rows = rows_loc * devices
    pieces = multiplier.reshape(1, rows_loc, devices, block_width)
    moved = lax.all_to_all(pieces, ("row", "col"), split_axis=2, concat_axis=0, tiled=True)
    direct = moved.reshape(all_rows, block_width)
    swapped = jnp.transpose(multiplier.reshape(virt_dev, OW, V, O), (2, 1, 0, 3)).reshape(
        all_rows, block_width
    )
    combined = 2.0 * direct - swapped
    partial_value = jnp.dot(
        lax.all_gather(combined, "col", axis=1, tiled=True),
        cycle_tiles,
        precision=lax.Precision.HIGHEST,
        preferred_element_type=jnp.float32,
    )
    partial_value = partial_value.reshape(all_rows, row_count, out_block)
    summed = lax.psum_scatter(partial_value, "row", scatter_dimension=1, tiled=True)
    own_cols = summed.reshape(all_rows, out_block)
    outgoing = own_cols.reshape(devices, rows_loc, 1, out_block)
    arrived = lax.all_to_all(outgoing, ("row", "col"), split_axis=0, concat_axis=2, tiled=True)
    own_rows = arrived.reshape(rows_loc, devices * out_block)
    mirrored = jnp.transpose(own_cols.reshape(V, OW, virt_dev, OW), (2, 1, 0, 3)).reshape(
        rows_loc, devices * out_block
    )
    return own_rows + mirrored


def solution(mesh):
    placed = (P(("row", "col"), None), P("row", "col"))
    return jax.shard_map(
        on_device, mesh=mesh, in_specs=placed, out_specs=P(("row", "col"), None), check_vma=False
    )
```

profile of v0, /device:TPU:0, one launch (start us, length us, event | category | flops | bytes accessed | tf_op | source)
XLA Modules:
  0.0 207.9 jit_solution(11825398114714194074)
XLA Ops:
  6.5 0.0 copy-start
  6.5 1.7 copy.18
  8.2 1.8 copy.11
  10.0 7.3 %all-to-all-start = ((f32[1,16,32,640]{3,1,0,2:T(8,128)}), f32[1,16,32,640]{3,1,0,2:T(8,128)S(1)}, u32[]{:S(2)}, u32[]{:S(2)}) async-start(f32[1,16,32,640]{3,1,0,2:T(8,128)} %copy.11), calls=%async_computation | async-start | bytes 2621440 | tf_op jit(solution)/shard_map/all_to_all | solution.py:21
  17.3 0.0 all-gather.2.cloned.1.call-start
  17.4 5.8 %reshape.26 = f32[16,1,512,40]{3,2,0,1:T(8,128)} reshape(f32[16,20480]{1,0:T(8,128)} %param.2) | data formatting | bytes 2621440 | tf_op jit(solution)/shard_map/reshape | solution.py:23
  23.2 3.6 %copy.13 = f32[512,1,16,40]{0,3,2,1:T(8,128)} copy(f32[512,1,16,40]{3,0,2,1:T(8,128)} %bitcast.34) | data formatting | bytes 2621440 | tf_op jit(solution)/shard_map/transpose | solution.py:23
  26.9 2.8 %copy.14 = f32[512,640]{1,0:T(8,128)} copy(f32[512,640]{0,1:T(8,128)} %bitcast.37) | data formatting | bytes 2621440 | tf_op jit(solution)/shard_map/reshape | solution.py:23
  29.7 20.9 %all-to-all-done = f32[1,16,32,640]{3,1,0,2:T(8,128)S(1)} async-done(((f32[1,16,32,640]{3,1,0,2:T(8,128)}), f32[1,16,32,640]{3,1,0,2:T(8,128)S(1)}, u32[]{:S(2)}, u32[]{:S(2)}) %all-to-all-start) | async-done | bytes 1310752 | tf_op jit(solution)/shard_map/all_to_all | solution.py:21
  50.5 0.0 copy-start.1
  50.5 0.1 bitcast_multiply_fusion
  50.6 1.2 copy-done.1
  51.9 1.2 bitcast_subtract_fusion
  53.1 0.0 all-gather.2.cloned.1.call-update
  53.1 0.0 reduce-scatter.4.cloned.1.call-start
  53.1 97.1 %all-gather.2.cloned.1.call-done = f32[512,5120]{1,0:T(8,128)} async-done(((f32[512,640]{1,0:T(8,128)}), f32[512,5120]{1,0:T(8,128)}) %all-gather.2.cloned.1.call-update) | async-done | bytes 10485776 | tf_op jit(solution)/shard_map/all_gather | solution.py:28
  150.3 0.0 copy-done
  150.3 13.4 %fusion = f32[512,64]{0,1:T(8,128)} fusion(f32[512,5120]{1,0:T(8,128)} %all-gather.2.cloned.1.call-done, f32[5120,64]{0,1:T(8,128)S(1)} %copy-done), kind=kOutput, calls=%fused_computation.4 | convolution fusion | flops 2013265920 | bytes 11927552 | tf_op jit(solution)/shard_map/dot_general | solution.py:27
  163.7 0.0 reduce-scatter.4.cloned.1.call-update
  163.7 22.3 %reduce-scatter.4.cloned.1.call-done = f32[512,1,16]{0,2,1:T(8,128)} async-done(((f32[512,4,16]{0,2,1:T(8,128)}), f32[512,1,16]{0,2,1:T(8,128)}) %reduce-scatter.4.cloned.1.call-update) | async-done | bytes 32784
  186.0 0.0 copy-start.2
  186.0 0.9 reshape_reshape.6
  187.0 0.2 copy.20
  187.2 0.1 reshape.32
  187.3 11.7 %all_to_all.24 = f32[32,1,256]{2,1,0:T(1,128)S(1)} all-to-all(f32[32,1,256]{2,1,0:T(1,128)S(1)} %reshape.32), channel_id=1, replica_groups=mesh['row'=4,'col'=8] {'row','col'}, dimensions={0} | all-to-all | bytes 65536 | tf_op jit(solution)/shard_map/all_to_all | solution.py:37
  199.0 0.5 broadcast.6
  199.5 0.7 reduce
  200.2 0.1 reshape.33
  200.3 0.1 copy.17
  200.4 0.0 copy-done.2
  200.4 0.6 bitcast_add_fusion
Async XLA Ops:
  6.5 143.7 %copy-start = (f32[5120,64]{0,1:T(8,128)S(1)}, f32[5120,64]{0,1:T(8,128)}, u32[]{:S(2)}) copy-start(f32[5120,64]{0,1:T(8,128)} %param.3) | copy-start | bytes 3932164
  10.0 40.5 %all-to-all-start = ((f32[1,16,32,640]{3,1,0,2:T(8,128)}), f32[1,16,32,640]{3,1,0,2:T(8,128)S(1)}, u32[]{:S(2)}, u32[]{:S(2)}) async-start(f32[1,16,32,640]{3,1,0,2:T(8,128)} %copy.11), calls=%async_computation | async-start | bytes 2621440 | tf_op jit(solution)/shard_map/all_to_all | solution.py:21
  17.3 132.9 %all-gather.2.cloned.1.call-start = ((), (), s32[]{:S(2)}) async-start(), calls=%async_computation.3 | async-start | bytes 11796480 | tf_op jit(solution)/shard_map/all_gather | solution.py:28
  50.5 1.3 copy-start.1
  53.1 133.0 %reduce-scatter.4.cloned.1.call-start = ((), (), s32[]{:S(2)}) async-start(), calls=%async_computation.4 | async-start | bytes 163840
  186.0 14.4 %copy-start.2 = (f32[512,1,16]{0,2,1:T(8,128)S(1)}, f32[512,1,16]{0,2,1:T(8,128)}, u32[]{:S(2)}) copy-start(f32[512,1,16]{0,2,1:T(8,128)} %reduce-scatter.4.cloned.1.call-done) | copy-start | bytes 98308
Sparse Core Ops, SparseCore 0:
  53.2 97.0 all-gather.1
  163.8 22.1 reduce-scatter.3
where the time goes:
time: 208 us
  waiting for transfers between devices  140 us (67%)
  local copies, waits for them, and re-layouts  19 us (9%)
  between operations  13.5 us (6%)
  matrix products  13.4 us (6%)
  blocking collectives  11.7 us (6%)
  starting transfers between devices  7.38 us (4%)
  other arithmetic  2.63 us (1%)
    all_gather x1, waiting for transfers between devices, on_device(): lax.all_gather(combined, 'col', axis=1, tiled=True)  97.1 us
    unnamed x3, waiting for transfers between devices  22.4 us
    all_to_all x1, waiting for transfers between devices, on_device(): lax.all_to_all(pieces, ('row', 'col'), split_axis=2, concat_axis=0, tiled...  20.9 us
    dot_general x1, matrix products, on_device(): jnp.dot(lax.all_gather(combined, 'col', axis=1, tiled=True), cycle_tiles,...  13.4 us
    all_to_all x1, blocking collectives, on_device(): lax.all_to_all(outgoing, ('row', 'col'), split_axis=0, concat_axis=2, til...  11.7 us
    all_to_all x1, starting transfers between devices, on_device(): lax.all_to_all(pieces, ('row', 'col'), split_axis=2, concat_axis=0, tiled...  7.3 us
    reshape x1, local copies, waits for them, and re-layouts, on_device(): multiplier.reshape(virt_dev, OW, V, O)  5.83 us
  transfers between devices with their start and end apart: 3, of which 3 were waited for; matrix products, arithmetic and copies ran while one was open for 6% of the time, Pallas kernels for 0%

commit v1 on v0

v1 whole, which is shorter than its diff:
```python
import jax
import jax.numpy as jnp
from jax import lax
from jax.sharding import PartitionSpec as P

O = 40
V = 512
OW = 1


def on_device(multiplier, cycle_tiles):
    rows_loc, full_width = multiplier.shape
    row_count = lax.axis_size("row")
    col_count = lax.axis_size("col")
    devices = row_count * col_count
    block_width = full_width // devices
    out_block = cycle_tiles.shape[1] // row_count
    virt_dev = rows_loc // OW
    all_rows = rows_loc * devices
    pieces = multiplier.reshape(1, rows_loc, devices, block_width)
    moved = lax.all_to_all(pieces, ("row", "col"), split_axis=2, concat_axis=0, tiled=True)
    direct = moved.reshape(all_rows, block_width)
    cycle_rows = lax.all_to_all(cycle_tiles.T, "col", split_axis=1, concat_axis=0, tiled=True)
    swapped = jnp.transpose(multiplier.reshape(virt_dev, OW, V, O), (2, 1, 0, 3)).reshape(
        all_rows, block_width
    )
    combined = 2.0 * direct - swapped
    partial_value = lax.dot_general(
        cycle_rows,
        combined,
        (((1,), (1,)), ((), ())),
        precision=lax.Precision.HIGHEST,
        preferred_element_type=jnp.float32,
    )
    partial_value = partial_value.reshape(col_count, row_count, out_block, all_rows)
    over_row = lax.psum_scatter(partial_value, "row", scatter_dimension=1, tiled=True)
    own_cols = lax.psum_scatter(over_row, "col", scatter_dimension=0, tiled=True)
    own_cols = own_cols.reshape(out_block, all_rows)
    outgoing = own_cols.reshape(1, out_block, devices, rows_loc)
    arrived = lax.all_to_all(outgoing, ("row", "col"), split_axis=2, concat_axis=0, tiled=True)
    own_rows = arrived.reshape(devices * out_block, rows_loc).T
    return own_rows + own_cols


def solution(mesh):
    placed = (P(("row", "col"), None), P("row", "col"))
    return jax.shard_map(
        on_device, mesh=mesh, in_specs=placed, out_specs=P(("row", "col"), None), check_vma=False
    )
```

time: 208 us -> 193 us (0.928)
  waiting for transfers between devices: 140 us -> 121 us
  matrix products: 13.4 us -> 3.7 us
  other arithmetic: 2.63 us -> 10.4 us
  local copies, waits for them, and re-layouts: 19 us -> 23.1 us
  starting transfers between devices: 7.38 us -> 10.9 us
    all_gather x1 -> x0, waiting for transfers between devices: 97.1 us -> none  [on_device(): lax.all_gather(combined, 'col', axis=1, tiled=True)]
    reduce_scatter x0 -> x1, waiting for transfers between devices: none -> 30.6 us  [on_device(): lax.psum_scatter(over_row, 'col', scatter_dimension=0, tiled=True)]
    unnamed x3, waiting for transfers between devices: 22.4 us -> 49.1 us
    all_to_all x1, waiting for transfers between devices: 20.9 us -> 32 us  [on_device(): lax.all_to_all(pieces, ('row', 'col'), split_axis=2, concat_axis=0, tiled...]
    dot_general x1, matrix products: 13.4 us -> 3.7 us  [on_device(): lax.dot_general(cycle_rows, combined, (((1,), (1,)), ((), ())), precision...]
    all_to_all x0 -> x1, waiting for transfers between devices: none -> 9.38 us  [on_device(): lax.all_to_all(cycle_tiles.T, 'col', split_axis=1, concat_axis=0, tiled=T...]
    sub x1, other arithmetic: 1.19 us -> 7.91 us  [on_device(): combined = 2.0 * direct - swapped]
    mul x0 -> x1, local copies, waits for them, and re-layouts: none -> 4.95 us  [on_device(): combined = 2.0 * direct - swapped]
  transfers between devices with their start and end apart: 3 -> 4, of which waited for: 3 -> 4; matrix products, arithmetic and copies ran while one was open for 6% -> 13% of each run, Pallas kernels for 0% -> 0%
where the time goes in v1:
time: 193 us; the launch traced here: 192 us
  waiting for transfers between devices  121 us (63%)
  local copies, waits for them, and re-layouts  23.1 us (12%)
  between operations  13.5 us (7%)
  starting transfers between devices  10.9 us (6%)
  other arithmetic  10.4 us (5%)
  blocking collectives  9.77 us (5%)
  matrix products  3.7 us (2%)
    unnamed x3, waiting for transfers between devices  49.1 us
    all_to_all x1, waiting for transfers between devices, on_device(): lax.all_to_all(pieces, ('row', 'col'), split_axis=2, concat_axis=0, tiled...  32 us
    reduce_scatter x1, waiting for transfers between devices, on_device(): lax.psum_scatter(over_row, 'col', scatter_dimension=0, tiled=True)  30.6 us
    all_to_all x1, blocking collectives, on_device(): lax.all_to_all(outgoing, ('row', 'col'), split_axis=2, concat_axis=0, til...  9.77 us
    all_to_all x1, waiting for transfers between devices, on_device(): lax.all_to_all(cycle_tiles.T, 'col', split_axis=1, concat_axis=0, tiled=T...  9.38 us
    sub x1, other arithmetic, on_device(): combined = 2.0 * direct - swapped  7.91 us
    all_to_all x1, starting transfers between devices, on_device(): lax.all_to_all(pieces, ('row', 'col'), split_axis=2, concat_axis=0, tiled...  7.3 us
    reshape x1, local copies, waits for them, and re-layouts, on_device(): multiplier.reshape(virt_dev, OW, V, O)  5.84 us
  transfers between devices with their start and end apart: 4, of which 4 were waited for; matrix products, arithmetic and copies ran while one was open for 13% of the time, Pallas kernels for 0%

profile of v1, /device:TPU:0, one launch (start us, length us, event | category | flops | bytes accessed | tf_op | source)
XLA Modules:
  0.0 192.5 jit_solution(2198952909515865545)
XLA Ops:
  6.5 1.6 copy.28
  8.1 1.8 copy.18
  9.9 0.0 copy-start
  9.9 7.3 %all-to-all-start = ((f32[1,16,32,640]{3,1,0,2:T(8,128)}), f32[1,16,32,640]{3,1,0,2:T(8,128)S(1)}, u32[]{:S(2)}, u32[]{:S(2)}) async-start(f32[1,16,32,640]{3,1,0,2:T(8,128)} %copy.18), calls=%async_computation | async-start | bytes 2621440 | tf_op jit(solution)/shard_map/all_to_all | solution.py:21
  17.3 0.0 copy-done
  17.3 1.2 copy.32
  18.5 32.0 %all-to-all-done = f32[1,16,32,640]{3,1,0,2:T(8,128)S(1)} async-done(((f32[1,16,32,640]{3,1,0,2:T(8,128)}), f32[1,16,32,640]{3,1,0,2:T(8,128)S(1)}, u32[]{:S(2)}, u32[]{:S(2)}) %all-to-all-start) | async-done | bytes 1310752 | tf_op jit(solution)/shard_map/all_to_all | solution.py:21
  50.5 3.6 %all-to-all-start.1 = ((f32[64,8,640]{2,0,1:T(8,128)}), f32[64,8,640]{2,0,1:T(8,128)S(1)}, u32[]{:S(2)}, u32[]{:S(2)}) async-start(f32[64,8,640]{2,0,1:T(8,128)} %bitcast.43), calls=%async_computation.1 | async-start | bytes 2621440 | tf_op jit(solution)/shard_map/all_to_all | solution.py:23
  54.0 0.0 all-reduce.3.cloned.1.call-start
  54.1 5.8 %reshape.38 = f32[16,1,512,40]{3,2,0,1:T(8,128)} reshape(f32[16,20480]{1,0:T(8,128)} %param.2) | data formatting | bytes 2621440 | tf_op jit(solution)/shard_map/reshape | solution.py:24
  59.9 1.2 multiply_bitcast_fusion
  61.1 4.9 %mul.26 = f32[512,1,16,40]{3,2,0,1:T(8,128)} reshape(f32[32,1,16,1,640]{4,2,0,3,1:T(8,128)} %multiply_bitcast_fusion) | data formatting | bytes 2621440 | tf_op jit(solution)/shard_map/mul | solution.py:27
  66.0 7.9 %bitcast_subtract_fusion = f32[512,1,16,40]{3,2,0,1:T(8,128)} fusion(f32[512,1,16,40]{3,2,0,1:T(8,128)} %mul.26, f32[16,1,512,40]{3,2,0,1:T(8,128)} %reshape.38), kind=kLoop, calls=%fused_computation | loop fusion | flops 327680 | bytes 3932160 | tf_op jit(solution)/shard_map/sub | solution.py:27
  74.0 2.8 %copy.20 = f32[512,1,16,40]{0,3,2,1:T(8,128)S(1)} copy(f32[512,1,16,40]{3,2,0,1:T(8,128)} %bitcast_subtract_fusion) | data formatting | bytes 2621440 | tf_op jit(solution)/shard_map/sub | solution.py:27
  76.8 9.4 %all-to-all-done.1 = f32[64,8,640]{2,0,1:T(8,128)S(1)} async-done(((f32[64,8,640]{2,0,1:T(8,128)}), f32[64,8,640]{2,0,1:T(8,128)S(1)}, u32[]{:S(2)}, u32[]{:S(2)}) %all-to-all-start.1) | async-done | bytes 1310752 | tf_op jit(solution)/shard_map/all_to_all | solution.py:23
  86.2 0.0 copy-start.2
  86.2 3.7 %fusion = f32[512,512]{0,1:T(8,128)} fusion(f32[512,640]{0,1:T(8,128)S(1)} %bitcast.46, f32[512,640]{1,0:T(8,128)S(1)} %bitcast.45), kind=kOutput, calls=%fused_computation.6 | convolution fusion | flops 2013265920 | bytes 3670016 | tf_op jit(solution)/shard_map/dot_general | solution.py:28
  89.9 0.0 all-reduce.3.cloned.1.call-update
  89.9 0.0 reduce-scatter.3.cloned.1.call-start
  89.9 0.0 copy-done.2
  90.0 0.6 dynamic-slice
  90.5 49.1 %all-reduce.3.cloned.1.call-done = f32[8,4,16,512]{3,2,1,0:T(8,128)} async-done(((f32[8,4,16,512]{3,2,1,0:T(8,128)}), f32[8,4,16,512]{3,2,1,0:T(8,128)}) %all-reduce.3.cloned.1.call-update) | async-done | bytes 1048592
  139.6 2.3 %constant_dynamic-slice_fusion = f32[8,1,16,512]{3,2,1,0:T(8,128)} fusion(f32[8,4,16,512]{3,2,1,0:T(8,128)} %all-reduce.3.cloned.1.call-done, u32[]{:T(128)} %bitcast.19), kind=kLoop, calls=%fused_computation.4 | loop fusion | bytes 524292
  141.9 0.0 reduce-scatter.3.cloned.1.call-update
  141.9 30.6 %reduce-scatter.3.cloned.1.call-done = f32[1,1,16,512]{3,2,1,0:T(8,128)} async-done(((f32[8,1,16,512]{3,2,1,0:T(8,128)}), f32[1,1,16,512]{3,2,1,0:T(8,128)}) %reduce-scatter.3.cloned.1.call-update) | async-done | bytes 32784 | tf_op jit(solution)/shard_map/reduce_scatter | solution.py:37
  172.5 0.0 copy-start.1
  172.5 0.9 reshape_reshape.3
  173.5 0.2 copy.33
  173.6 0.1 reshape.45
  173.8 9.8 %all_to_all.43 = f32[32,1,256]{2,1,0:T(1,128)S(1)} all-to-all(f32[32,1,256]{2,1,0:T(1,128)S(1)} %reshape.45), channel_id=1, replica_groups=mesh['row'=4,'col'=8] {'row','col'}, dimensions={0} | all-to-all | bytes 65536 | tf_op jit(solution)/shard_map/all_to_all | solution.py:40
  183.5 0.5 broadcast.13
  184.1 0.7 reduce
  184.8 0.1 reshape.46
  184.9 0.1 copy.24
  185.0 0.0 copy-done.1
  185.0 0.6 bitcast_add_fusion
Async XLA Ops:
  9.9 7.3 %copy-start = (f32[5120,64]{0,1:T(8,128)S(1)}, f32[5120,64]{0,1:T(8,128)}, u32[]{:S(2)}) copy-start(f32[5120,64]{0,1:T(8,128)} %param.3) | copy-start | bytes 3932164
  9.9 40.5 %all-to-all-start = ((f32[1,16,32,640]{3,1,0,2:T(8,128)}), f32[1,16,32,640]{3,1,0,2:T(8,128)S(1)}, u32[]{:S(2)}, u32[]{:S(2)}) async-start(f32[1,16,32,640]{3,1,0,2:T(8,128)} %copy.18), calls=%async_computation | async-start | bytes 2621440 | tf_op jit(solution)/shard_map/all_to_all | solution.py:21
  50.5 35.7 %all-to-all-start.1 = ((f32[64,8,640]{2,0,1:T(8,128)}), f32[64,8,640]{2,0,1:T(8,128)S(1)}, u32[]{:S(2)}, u32[]{:S(2)}) async-start(f32[64,8,640]{2,0,1:T(8,128)} %bitcast.43), calls=%async_computation.1 | async-start | bytes 2621440 | tf_op jit(solution)/shard_map/all_to_all | solution.py:23
  54.0 85.6 %all-reduce.3.cloned.1.call-start = ((), (), s32[]{:S(2)}) async-start(), calls=%async_computation.5 | async-start | bytes 2097152
  86.2 3.8 %copy-start.2 = (u32[32]{0:T(128)S(1)}, u32[32]{0:T(128)}, u32[]{:S(2)}) copy-start(u32[32]{0:T(128)} %constant.5) | copy-start | bytes 388
  89.9 82.6 %reduce-scatter.3.cloned.1.call-start = ((), (), s32[]{:S(2)}) async-start(), calls=%async_computation.4 | async-start | bytes 294912 | tf_op jit(solution)/shard_map/reduce_scatter | solution.py:37
  172.5 12.5 %copy-start.1 = (f32[1,1,16,512]{3,2,1,0:T(8,128)S(1)}, f32[1,1,16,512]{3,2,1,0:T(8,128)}, u32[]{:S(2)}) copy-start(f32[1,1,16,512]{3,2,1,0:T(8,128)} %reduce-scatter.3.cloned.1.call-done) | copy-start | bytes 98308
Sparse Core Ops, SparseCore 0:
  90.0 49.5 all-reduce.2
  142.1 30.3 reduce-scatter.2

commit v2 on v1

--- a/solution.py
+++ b/solution.py
@@ -1,14 +1,280 @@
+import functools
+
 import jax
 import jax.numpy as jnp
 from jax import lax
+from jax.experimental import pallas as pl
+from jax.experimental.pallas import tpu as pltpu
 from jax.sharding import PartitionSpec as P
 
 O = 40
 V = 512
 OW = 1
-
-
-def on_device(multiplier, cycle_tiles):
+MESH = pl.DeviceIdType.MESH
+
+
+def flip(x, y, size):
+    total, bit = 0, 1
+    while bit < size:
+        total = total + bit * ((x // bit + y // bit) % 2)
+        bit *= 2
+    return total
+
+
+def halves(x):
+    high = x.astype(jnp.bfloat16)
+    return high, (x - high.astype(jnp.float32)).astype(jnp.bfloat16)
+
+
+def dot_nt(x, y):
+    return lax.dot_general(
+        x, y, (((1,), (1,)), ((), ())), preferred_element_type=jnp.float32
+    )
+
+
+def cycle_kernel(
+    rows, cols, t_ref, w_ref, out_ref,
+    wt, tdir, u, sw, dh, dl, wr, pbuf, rbuf, qbuf, cbuf, qt, mbuf,
+    t_send, t_recv, w_send, w_recv, r_send, r_recv, c_send, c_recv, m_send, m_recv,
+):
+    n = rows * cols
+    own, width = t_ref.shape
+    block = width // n
+    chunk = w_ref.shape[1]
+    count = own * n
+    r = lax.axis_index("row")
+    c = lax.axis_index("col")
+    me = r * cols + c
+
+    def partner(step):
+        s, q = step % cols, step // cols
+        pr = flip(r, (q + s) % rows, rows)
+        pc = flip(c, (s % 2) * (cols // 2) + s // 2, cols)
+        return pr, pc, pr * cols + pc
+
+    barrier = pltpu.get_barrier_semaphore()
+
+    @pl.loop(1, n)
+    def _(step):
+        pr, pc, _ = partner(step)
+        pl.semaphore_signal(barrier, inc=1, device_id=(pr, pc), device_id_type=MESH)
+
+    pl.semaphore_wait(barrier, n - 1)
+
+    def t_copy(sender, pr, pc, dest):
+        return pltpu.make_async_remote_copy(
+            src_ref=t_ref.at[:, pl.ds(pl.multiple_of(dest * block, 128), block)],
+            dst_ref=tdir.at[pl.ds(pl.multiple_of(sender * own, own), own), :],
+            send_sem=t_send.at[dest],
+            recv_sem=t_recv.at[sender],
+            device_id=(pr, pc),
+            device_id_type=MESH,
+        )
+
+    @pl.loop(1, n)
+    def _(step):
+        pr, pc, dest = partner(step)
+        t_copy(me, pr, pc, dest).start()
+
+    def w_block(pc):
+        return w_ref[pl.ds(pl.multiple_of(pc * block, 128), block), :].T
+
+    def w_copy(sender, dest):
+        return pltpu.make_async_remote_copy(
+            src_ref=wt.at[dest],
+            dst_ref=wr.at[sender],
+            send_sem=w_send.at[dest],
+            recv_sem=w_recv.at[sender],
+            device_id=(r, dest),
+            device_id_type=MESH,
+        )
+
+    @pl.loop(1, cols)
+    def _(step):
+        _, pc, _ = partner(step)
+        wt[pc] = w_block(pc)
+        w_copy(c, pc).start()
+
+    wr[c] = w_block(c)
+    tdir[pl.ds(pl.multiple_of(me * own, own), own), :] = t_ref[
+        :, pl.ds(pl.multiple_of(me * block, 128), block)
+    ]
+
+    @pl.loop(0, n)
+    def _(part):
+        x = t_ref[:, pl.ds(pl.multiple_of(part * block, 128), block)]
+        for j in range(own):
+            piece = jnp.pad(x[:, j * O : (j + 1) * O], ((0, 0), (0, 128 - O)))
+            for half in range(0, own, 8):
+                u[pl.ds(half * count + part * own + j, 8, stride=count), :] = piece[
+                    half : half + 8
+                ]
+
+    for j in range(own):
+        sw[:, j * O : (j + 1) * O] = u[j * count : (j + 1) * count, 0:O]
+
+    def combine(source):
+        at = pl.ds(pl.multiple_of(source * own, own), own)
+        high, low = halves(2.0 * tdir[at, :] - sw[at, :])
+        dh[at, :] = high
+        dl[at, :] = low
+
+    combine(me)
+
+    @pl.loop(1, n)
+    def _(step):
+        pr, pc, source = partner(step)
+        t_copy(source, pr, pc, me).wait_recv()
+        combine(source)
+
+    def r_copy(pc, sender, dest):
+        return pltpu.make_async_remote_copy(
+            src_ref=pbuf.at[pc, pl.ds(pl.multiple_of(dest * own, own), own), :],
+            dst_ref=rbuf.at[pc, sender],
+            send_sem=r_send.at[pc, dest],
+            recv_sem=r_recv.at[pc, sender],
+            device_id=(dest, c),
+            device_id_type=MESH,
+        )
+
+    def c_copy(sender, dest):
+        return pltpu.make_async_remote_copy(
+            src_ref=qbuf.at[dest],
+            dst_ref=cbuf.at[sender],
+            send_sem=c_send.at[dest],
+            recv_sem=c_recv.at[sender],
+            device_id=(r, dest),
+            device_id_type=MESH,
+        )
+
+    def multiply(pc):
+        high, low = halves(wr[pc])
+        both = dot_nt(jnp.concatenate([high, low], axis=0), dh[...])
+        pbuf[pc] = both[:chunk] + both[chunk:] + dot_nt(high, dl[...])
+        for i in range(1, rows):
+            dest = (r + i) % rows
+            r_copy(pc, r, dest).start()
+
+    def collect(pc):
+        total = pbuf[pc, pl.ds(pl.multiple_of(r * own, own), own), :]
+        for i in range(1, rows):
+            sender = (r + i) % rows
+            r_copy(pc, sender, r).wait_recv()
+            total = total + rbuf[pc, sender]
+        qbuf[pc] = total
+
+    multiply(c)
+
+    @pl.loop(1, cols)
+    def _(step):
+        _, pc, _ = partner(step)
+        w_copy(pc, c).wait_recv()
+        multiply(pc)
+        _, before, _ = partner(step - 1)
+        collect(before)
+
+        @pl.when(step > 1)
+        def _():
+            c_copy(c, before).start()
+
+    _, last, _ = partner(cols - 1)
+    collect(last)
+    c_copy(c, last).start()
+
+    qt[...] = qbuf[...].reshape(cols * own, count).T
+
+    def m_copy(sender, pr, pc, dest):
+        return pltpu.make_async_remote_copy(
+            src_ref=qt.at[pl.ds(pl.multiple_of(dest * own, own), own), :],
+            dst_ref=mbuf.at[sender],
+            send_sem=m_send.at[dest],
+            recv_sem=m_recv.at[sender],
+            device_id=(pr, pc),
+            device_id_type=MESH,
+        )
+
+    @pl.loop(1, n)
+    def _(step):
+        pr, pc, dest = partner(step)
+        m_copy(me, pr, pc, dest).start()
+
+    mbuf[me] = qt[pl.ds(pl.multiple_of(me * own, own), own), :]
+    cbuf[c] = qbuf[c]
+
+    @pl.loop(1, cols)
+    def _(step):
+        _, pc, _ = partner(step)
+        c_copy(pc, c).wait_recv()
+
+    @pl.loop(1, n)
+    def _(step):
+        pr, pc, source = partner(step)
+        m_copy(source, pr, pc, me).wait_recv()
+
+    mirrored = jnp.sum(cbuf[...], axis=0)
+    lanes = cols * own
+    for i in range(rows):
+        at = slice(i * lanes, (i + 1) * lanes)
+        out_ref[:, at] = mirrored[:, at] + jnp.sum(mbuf[i * cols : (i + 1) * cols], axis=0)
+
+    @pl.loop(1, n)
+    def _(step):
+        pr, pc, dest = partner(step)
+        t_copy(me, pr, pc, dest).wait_send()
+        m_copy(me, pr, pc, dest).wait_send()
+
+    @pl.loop(1, cols)
+    def _(step):
+        _, pc, _ = partner(step)
+        w_copy(c, pc).wait_send()
+        c_copy(c, pc).wait_send()
+
+    @pl.loop(0, cols)
+    def _(pc):
+        for i in range(1, rows):
+            r_copy(pc, r, (r + i) % rows).wait_send()
+
+
+def in_one_kernel(multiplier, cycle_tiles):
+    own, width = multiplier.shape
+    rows, cols = lax.axis_size("row"), lax.axis_size("col")
+    n = rows * cols
+    block, chunk, count = width // n, cycle_tiles.shape[1], own * n
+    f32, bf16 = jnp.float32, jnp.bfloat16
+    dma = pltpu.SemaphoreType.DMA
+    return pl.pallas_call(
+        functools.partial(cycle_kernel, rows, cols),
+        out_shape=jax.ShapeDtypeStruct((own, count), f32),
+        in_specs=[pl.BlockSpec(memory_space=pltpu.VMEM)] * 2,
+        out_specs=pl.BlockSpec(memory_space=pltpu.VMEM),
+        scratch_shapes=[
+            pltpu.VMEM((cols, chunk, block), f32),
+            pltpu.VMEM((count, block), f32),
+            pltpu.VMEM((own * count, 128), f32),
+            pltpu.VMEM((count, block), f32),
+            pltpu.VMEM((count, block), bf16),
+            pltpu.VMEM((count, block), bf16),
+            pltpu.VMEM((cols, chunk, block), f32),
+            pltpu.VMEM((cols, chunk, count), f32),
+            pltpu.VMEM((cols, rows, own, count), f32),
+            pltpu.VMEM((cols, own, count), f32),
+            pltpu.VMEM((cols, own, count), f32),
+            pltpu.VMEM((count, cols * own), f32),
+            pltpu.VMEM((n, own, cols * own), f32),
+            dma((n,)), dma((n,)), dma((cols,)), dma((cols,)),
+            dma((cols, rows)), dma((cols, rows)),
+            dma((cols,)), dma((cols,)), dma((n,)), dma((n,)),
+        ],
+        compiler_params=pltpu.CompilerParams(
+            collective_id=0, has_side_effects=True, vmem_limit_bytes=48 * 1024 * 1024
+        ),
+        cost_estimate=pl.CostEstimate(
+            flops=6 * count * block * count, bytes_accessed=4 * own * width, transcendentals=0
+        ),
+    )(multiplier, cycle_tiles)
+
+
+def in_collectives(multiplier, cycle_tiles):
     rows_loc, full_width = multiplier.shape
     row_count = lax.axis_size("row")
     col_count = lax.axis_size("col")
@@ -42,6 +308,17 @@
     return own_rows + own_cols
 
 
+def on_device(multiplier, cycle_tiles):
+    own, width = multiplier.shape
+    rows, cols = lax.axis_size("row"), lax.axis_size("col")
+    block = width // (rows * cols)
+    powers = rows & (rows - 1) == 0 and cols & (cols - 1) == 0
+    whole_tiles = own % 16 == 0 and block % 128 == 0 and (cols * own) % 128 == 0
+    if OW == 1 and O <= 128 and powers and whole_tiles and block == own * O:
+        return in_one_kernel(multiplier, cycle_tiles)
+    return in_collectives(multiplier, cycle_tiles)
+
+
 def solution(mesh):
     placed = (P(("row", "col"), None), P("row", "col"))
     return jax.shard_map(

time: 193 us -> 87.4 us (0.45)
  waiting for transfers between devices: 121 us -> 0 us
  Pallas kernels: 0 us -> 83.4 us
  local copies, waits for them, and re-layouts: 23.1 us -> 3.84 us
  between operations: 13.5 us -> 0.03 us
  starting transfers between devices: 10.9 us -> 0 us
  other arithmetic: 10.4 us -> 0 us
  blocking collectives: 9.77 us -> 0 us
  matrix products: 3.7 us -> 0 us
    pallas_call x0 -> x1, Pallas kernels: none -> 83.4 us  [in_one_kernel(): pl.pallas_call(functools.partial(cycle_kernel, rows, cols), out_shape=jax...]
    unnamed x3 -> x0, waiting for transfers between devices: 49.1 us -> none
    all_to_all x2 -> x0, waiting for transfers between devices: 41.3 us -> none  [the longest x1 32 us: on_device(): lax.all_to_all(pieces, ('row', 'col'), split_axis=2, concat_axis=0, tiled...]
    reduce_scatter x1 -> x0, waiting for transfers between devices: 30.6 us -> none  [on_device(): lax.psum_scatter(over_row, 'col', scatter_dimension=0, tiled=True)]
    all_to_all x2 -> x0, starting transfers between devices: 10.9 us -> none  [the longest x1 7.3 us: on_device(): lax.all_to_all(pieces, ('row', 'col'), split_axis=2, concat_axis=0, tiled...]
    all_to_all x1 -> x0, blocking collectives: 9.77 us -> none  [on_device(): lax.all_to_all(outgoing, ('row', 'col'), split_axis=2, concat_axis=0, til...]
    sub x1 -> x0, other arithmetic: 7.91 us -> none  [on_device(): combined = 2.0 * direct - swapped]
    reshape x3 -> x0, local copies, waits for them, and re-layouts: 7.77 us -> none  [the longest x1 5.84 us: on_device(): multiplier.reshape(virt_dev, OW, V, O)]
  transfers between devices with their start and end apart: 4 -> 0, of which waited for: 4 -> 0; matrix products, arithmetic and copies ran while one was open for 13% -> 0% of each run, Pallas kernels for 0% -> 0%
where the time goes in v2:
time: 87.4 us; the launch traced here: 87.2 us
  Pallas kernels  83.4 us (95%)
  local copies, waits for them, and re-layouts  3.84 us (4%)
    pallas_call x1, Pallas kernels, in_one_kernel(): pl.pallas_call(functools.partial(cycle_kernel, rows, cols), out_shape=jax...  83.4 us
    unnamed x4, local copies, waits for them, and re-layouts  3.84 us

profile of v2, /device:TPU:0, one launch (start us, length us, event | category | flops | bytes accessed | tf_op | source)
XLA Modules:
  0.0 87.2 jit_solution(1298329386543368634)
XLA Ops:
  0.0 1.9 %copy.3.w_ref = f32[5120,64]{1,0:T(8,128)S(1)} copy(f32[5120,64]{0,1:T(8,128)} %param.3) | data formatting | bytes 2621440 | tf_op args[1]
  1.9 0.0 copy-start
  1.9 1.3 %copy-done = f32[16,20480]{1,0:T(8,128)S(1)} copy-done((f32[16,20480]{1,0:T(8,128)S(1)}, f32[16,20480]{1,0:T(8,128)}, u32[]{:S(2)}) %copy-start) | copy-done | bytes 1310744
  3.2 83.4 %shard_map.28 = f32[16,512]{1,0:T(8,128)S(1)} custom-call(f32[16,20480]{1,0:T(8,128)S(1)} %copy-done, f32[5120,64]{1,0:T(8,128)S(1)} %copy.3.w_ref), custom_call_target="tpu_custom_call" | custom-call | flops 1006632960 | bytes 1310720 | tf_op jit(solution)/shard_map/pallas_call | solution.py:245
  86.6 0.6 copy.5
Async XLA Ops:
  1.9 1.3 %copy-start = (f32[16,20480]{1,0:T(8,128)S(1)}, f32[16,20480]{1,0:T(8,128)}, u32[]{:S(2)}) copy-start(f32[16,20480]{1,0:T(8,128)} %t_ref.1) | copy-start | bytes 3932164

commit v3 on v2

--- a/solution.py
+++ b/solution.py
@@ -33,23 +33,35 @@
 
 
 def cycle_kernel(
-    rows, cols, t_ref, w_ref, out_ref,
-    wt, tdir, u, sw, dh, dl, wr, pbuf, rbuf, qbuf, cbuf, qt, mbuf,
-    t_send, t_recv, w_send, w_recv, r_send, r_recv, c_send, c_recv, m_send, m_recv,
+    rows, cols, t_hbm, w_hbm, out_ref,
+    t_ref, tdir, u, sw, dh, dl, wr, pbuf, rbuf, qbuf, cbuf, tall, fbuf, fr, flat,
+    here, t_send, t_recv, w_send, w_recv, r_send, r_recv, c_send, c_recv, f_send, f_recv,
 ):
     n = rows * cols
     own, width = t_ref.shape
     block = width // n
-    chunk = w_ref.shape[1]
+    chunk = w_hbm.shape[0]
     count = own * n
     r = lax.axis_index("row")
     c = lax.axis_index("col")
     me = r * cols + c
 
+    core = c % 2
+    t_here = pltpu.make_async_copy(t_hbm, t_ref, here.at[0])
+    t_here.start()
+    w_here = pltpu.make_async_copy(
+        w_hbm.at[:, pl.ds(pl.multiple_of(c * block, 128), block)], wr.at[c], here.at[1]
+    )
+    w_here.start()
+
+    def mask_of(step):
+        s = step % cols
+        return (s % 2) * (cols // 2) + s // 2
+
     def partner(step):
         s, q = step % cols, step // cols
         pr = flip(r, (q + s) % rows, rows)
-        pc = flip(c, (s % 2) * (cols // 2) + s // 2, cols)
+        pc = flip(c, mask_of(step), cols)
         return pr, pc, pr * cols + pc
 
     barrier = pltpu.get_barrier_semaphore()
@@ -63,7 +75,7 @@
 
     def t_copy(sender, pr, pc, dest):
         return pltpu.make_async_remote_copy(
-            src_ref=t_ref.at[:, pl.ds(pl.multiple_of(dest * block, 128), block)],
+            src_ref=t_hbm.at[:, pl.ds(pl.multiple_of(dest * block, 128), block)],
             dst_ref=tdir.at[pl.ds(pl.multiple_of(sender * own, own), own), :],
             send_sem=t_send.at[dest],
             recv_sem=t_recv.at[sender],
@@ -76,12 +88,9 @@
         pr, pc, dest = partner(step)
         t_copy(me, pr, pc, dest).start()
 
-    def w_block(pc):
-        return w_ref[pl.ds(pl.multiple_of(pc * block, 128), block), :].T
-
     def w_copy(sender, dest):
         return pltpu.make_async_remote_copy(
-            src_ref=wt.at[dest],
+            src_ref=w_hbm.at[:, pl.ds(pl.multiple_of(dest * block, 128), block)],
             dst_ref=wr.at[sender],
             send_sem=w_send.at[dest],
             recv_sem=w_recv.at[sender],
@@ -92,10 +101,9 @@
     @pl.loop(1, cols)
     def _(step):
         _, pc, _ = partner(step)
-        wt[pc] = w_block(pc)
         w_copy(c, pc).start()
 
-    wr[c] = w_block(c)
+    t_here.wait()
     tdir[pl.ds(pl.multiple_of(me * own, own), own), :] = t_ref[
         :, pl.ds(pl.multiple_of(me * block, 128), block)
     ]
@@ -127,22 +135,22 @@
         t_copy(source, pr, pc, me).wait_recv()
         combine(source)
 
-    def r_copy(pc, sender, dest):
+    def r_copy(pc, sender_row, sender_core, dest):
         return pltpu.make_async_remote_copy(
             src_ref=pbuf.at[pc, pl.ds(pl.multiple_of(dest * own, own), own), :],
-            dst_ref=rbuf.at[pc, sender],
+            dst_ref=rbuf.at[pc // 2, sender_row, sender_core],
             send_sem=r_send.at[pc, dest],
-            recv_sem=r_recv.at[pc, sender],
-            device_id=(dest, c),
+            recv_sem=r_recv.at[pc // 2, sender_row, sender_core],
+            device_id=(dest, c - core + pc % 2),
             device_id_type=MESH,
         )
 
     def c_copy(sender, dest):
         return pltpu.make_async_remote_copy(
-            src_ref=qbuf.at[dest],
-            dst_ref=cbuf.at[sender],
-            send_sem=c_send.at[dest],
-            recv_sem=c_recv.at[sender],
+            src_ref=qbuf.at[dest // 2],
+            dst_ref=cbuf.at[sender // 2],
+            send_sem=c_send.at[dest // 2],
+            recv_sem=c_recv.at[sender // 2],
             device_id=(r, dest),
             device_id_type=MESH,
         )
@@ -152,17 +160,33 @@
         both = dot_nt(jnp.concatenate([high, low], axis=0), dh[...])
         pbuf[pc] = both[:chunk] + both[chunk:] + dot_nt(high, dl[...])
         for i in range(1, rows):
-            dest = (r + i) % rows
-            r_copy(pc, r, dest).start()
+            r_copy(pc, r, core, (r + i) % rows).start()
+
+        @pl.when(pc % 2 != core)
+        def _():
+            r_copy(pc, r, core, r).start()
 
     def collect(pc):
         total = pbuf[pc, pl.ds(pl.multiple_of(r * own, own), own), :]
-        for i in range(1, rows):
-            sender = (r + i) % rows
-            r_copy(pc, sender, r).wait_recv()
-            total = total + rbuf[pc, sender]
-        qbuf[pc] = total
-
+        for i in range(rows):
+            for k in range(2):
+                if i or k:
+                    sender, side = (r + i) % rows, (core + k) % 2
+                    r_copy(pc, sender, side, r).wait_recv()
+                    total = total + rbuf[pc // 2, sender, side]
+        qbuf[pc // 2] = total
+
+    steps = [mask_of(step) for step in range(cols)]
+    ready = {m: max(steps.index(m), steps.index(m + 1)) + 1 for m in range(0, cols, 2)}
+    order = sorted(ready, key=lambda m: ready[m])
+
+    def collect_mask(mask):
+        pc = flip(c, mask, cols)
+        collect(pc)
+        if mask:
+            c_copy(c, pc).start()
+
+    w_here.wait()
     multiply(c)
 
     @pl.loop(1, cols)
@@ -170,25 +194,36 @@
         _, pc, _ = partner(step)
         w_copy(pc, c).wait_recv()
         multiply(pc)
-        _, before, _ = partner(step - 1)
-        collect(before)
-
-        @pl.when(step > 1)
-        def _():
-            c_copy(c, before).start()
-
-    _, last, _ = partner(cols - 1)
-    collect(last)
-    c_copy(c, last).start()
-
-    qt[...] = qbuf[...].reshape(cols * own, count).T
-
-    def m_copy(sender, pr, pc, dest):
-        return pltpu.make_async_remote_copy(
-            src_ref=qt.at[pl.ds(pl.multiple_of(dest * own, own), own), :],
-            dst_ref=mbuf.at[sender],
-            send_sem=m_send.at[dest],
-            recv_sem=m_recv.at[sender],
+        for mask in order:
+            if ready[mask] < cols:
+                pl.when(step == ready[mask])(functools.partial(collect_mask, mask))
+
+    for mask in order:
+        if ready[mask] >= cols:
+            collect_mask(mask)
+
+    full = qbuf[c // 2]
+    for mask in order:
+        if mask:
+            pc = flip(c, mask, cols)
+            c_copy(pc, c).wait_recv()
+            full = full + cbuf[pc // 2]
+
+    per = 128 // own
+    parts = own // per
+    tall[...] = jnp.pad(full.T, ((0, 0), (0, 128 - own)))
+    packed = jnp.concatenate(
+        [tall[pl.ds(j, n * parts, stride=per), :][:, :own] for j in range(per)], axis=1
+    )
+    for d in range(n):
+        fbuf[d] = packed[d * parts : (d + 1) * parts]
+
+    def f_copy(sender, pr, pc, dest):
+        return pltpu.make_async_remote_copy(
+            src_ref=fbuf.at[dest],
+            dst_ref=fr.at[sender],
+            send_sem=f_send.at[dest],
+            recv_sem=f_recv.at[sender],
             device_id=(pr, pc),
             device_id_type=MESH,
         )
@@ -196,43 +231,52 @@
     @pl.loop(1, n)
     def _(step):
         pr, pc, dest = partner(step)
-        m_copy(me, pr, pc, dest).start()
-
-    mbuf[me] = qt[pl.ds(pl.multiple_of(me * own, own), own), :]
-    cbuf[c] = qbuf[c]
-
-    @pl.loop(1, cols)
-    def _(step):
-        _, pc, _ = partner(step)
-        c_copy(pc, c).wait_recv()
-
-    @pl.loop(1, n)
-    def _(step):
-        pr, pc, source = partner(step)
-        m_copy(source, pr, pc, me).wait_recv()
-
-    mirrored = jnp.sum(cbuf[...], axis=0)
-    lanes = cols * own
-    for i in range(rows):
-        at = slice(i * lanes, (i + 1) * lanes)
-        out_ref[:, at] = mirrored[:, at] + jnp.sum(mbuf[i * cols : (i + 1) * cols], axis=0)
+        f_copy(me, pr, pc, dest).start()
+
+    fr[me] = fbuf[me]
 
     @pl.loop(1, n)
     def _(step):
         pr, pc, dest = partner(step)
         t_copy(me, pr, pc, dest).wait_send()
-        m_copy(me, pr, pc, dest).wait_send()
 
     @pl.loop(1, cols)
     def _(step):
         _, pc, _ = partner(step)
         w_copy(c, pc).wait_send()
-        c_copy(c, pc).wait_send()
+
+    for mask in order:
+        if mask:
+            c_copy(c, flip(c, mask, cols)).wait_send()
 
     @pl.loop(0, cols)
     def _(pc):
         for i in range(1, rows):
-            r_copy(pc, r, (r + i) % rows).wait_send()
+            r_copy(pc, r, core, (r + i) % rows).wait_send()
+
+        @pl.when(pc % 2 != core)
+        def _():
+            r_copy(pc, r, core, r).wait_send()
+
+    @pl.loop(1, n)
+    def _(step):
+        pr, pc, source = partner(step)
+        f_copy(source, pr, pc, me).wait_recv()
+
+    for d in range(n):
+        flat[d * parts : (d + 1) * parts, :] = fr[d]
+    got = flat[...]
+    for j in range(per):
+        tall[pl.ds(j, n * parts, stride=per), :] = jnp.pad(
+            got[:, j * own : (j + 1) * own], ((0, 0), (0, 128 - own))
+        )
+    across = jnp.concatenate([tall[d * own : (d + 1) * own, :own] for d in range(n)], axis=1)
+    out_ref[...] = full + across
+
+    @pl.loop(1, n)
+    def _(step):
+        pr, pc, dest = partner(step)
+        f_copy(me, pr, pc, dest).wait_send()
 
 
 def in_one_kernel(multiplier, cycle_tiles):
@@ -240,15 +284,16 @@
     rows, cols = lax.axis_size("row"), lax.axis_size("col")
     n = rows * cols
     block, chunk, count = width // n, cycle_tiles.shape[1], own * n
+    parts = own * own // 128
     f32, bf16 = jnp.float32, jnp.bfloat16
     dma = pltpu.SemaphoreType.DMA
     return pl.pallas_call(
         functools.partial(cycle_kernel, rows, cols),
         out_shape=jax.ShapeDtypeStruct((own, count), f32),
-        in_specs=[pl.BlockSpec(memory_space=pltpu.VMEM)] * 2,
+        in_specs=[pl.BlockSpec(memory_space=pltpu.HBM)] * 2,
         out_specs=pl.BlockSpec(memory_space=pltpu.VMEM),
         scratch_shapes=[
-            pltpu.VMEM((cols, chunk, block), f32),
+            pltpu.VMEM((own, width), f32),
             pltpu.VMEM((count, block), f32),
             pltpu.VMEM((own * count, 128), f32),
             pltpu.VMEM((count, block), f32),
@@ -256,22 +301,24 @@
             pltpu.VMEM((count, block), bf16),
             pltpu.VMEM((cols, chunk, block), f32),
             pltpu.VMEM((cols, chunk, count), f32),
-            pltpu.VMEM((cols, rows, own, count), f32),
-            pltpu.VMEM((cols, own, count), f32),
-            pltpu.VMEM((cols, own, count), f32),
-            pltpu.VMEM((count, cols * own), f32),
-            pltpu.VMEM((n, own, cols * own), f32),
-            dma((n,)), dma((n,)), dma((cols,)), dma((cols,)),
-            dma((cols, rows)), dma((cols, rows)),
-            dma((cols,)), dma((cols,)), dma((n,)), dma((n,)),
+            pltpu.VMEM((cols // 2, rows, 2, own, count), f32),
+            pltpu.VMEM((cols // 2, own, count), f32),
+            pltpu.VMEM((cols // 2, own, count), f32),
+            pltpu.VMEM((count, 128), f32),
+            pltpu.VMEM((n, parts, 128), f32),
+            pltpu.VMEM((n, parts, 128), f32),
+            pltpu.VMEM((n * parts, 128), f32),
+            dma((2,)), dma((n,)), dma((n,)), dma((cols,)), dma((cols,)),
+            dma((cols, rows)), dma((cols // 2, rows, 2)),
+            dma((cols // 2,)), dma((cols // 2,)), dma((n,)), dma((n,)),
         ],
         compiler_params=pltpu.CompilerParams(
-            collective_id=0, has_side_effects=True, vmem_limit_bytes=48 * 1024 * 1024
+            collective_id=0, has_side_effects=True, vmem_limit_bytes=62 * 1024 * 1024
         ),
         cost_estimate=pl.CostEstimate(
             flops=6 * count * block * count, bytes_accessed=4 * own * width, transcendentals=0
         ),
-    )(multiplier, cycle_tiles)
+    )(multiplier, cycle_tiles.T)
 
 
 def in_collectives(multiplier, cycle_tiles):
@@ -313,7 +360,7 @@
     rows, cols = lax.axis_size("row"), lax.axis_size("col")
     block = width // (rows * cols)
     powers = rows & (rows - 1) == 0 and cols & (cols - 1) == 0
-    whole_tiles = own % 16 == 0 and block % 128 == 0 and (cols * own) % 128 == 0
+    whole_tiles = own % 16 == 0 and 128 % own == 0 and block % 128 == 0 and cols > 1
     if OW == 1 and O <= 128 and powers and whole_tiles and block == own * O:
         return in_one_kernel(multiplier, cycle_tiles)
     return in_collectives(multiplier, cycle_tiles)

time: 87.4 us -> 85.8 us (0.982)
  local copies, waits for them, and re-layouts: 3.84 us -> 1.38 us
    unnamed x4 -> x1, local copies, waits for them, and re-layouts: 3.84 us -> 1.38 us
where the time goes in v3:
time: 85.8 us; the launch traced here: 85.6 us
  Pallas kernels  84.2 us (98%)
  local copies, waits for them, and re-layouts  1.38 us (2%)
    pallas_call x1, Pallas kernels, in_one_kernel(): pl.pallas_call(functools.partial(cycle_kernel, rows, cols), out_shape=jax...  84.2 us

profile of v3, /device:TPU:0, one launch (start us, length us, event | category | flops | bytes accessed | tf_op | source)
XLA Modules:
  0.0 85.6 jit_solution(4752864033908769645)
XLA Ops:
  0.0 84.2 %shard_map.28 = f32[16,512]{1,0:T(8,128)} custom-call(f32[16,20480]{1,0:T(8,128)} %t_hbm.1, f32[64,5120]{1,0:T(8,128)} %bitcast.1), custom_call_target="tpu_custom_call" | custom-call | flops 1006632960 | bytes 1310720 | tf_op jit(solution)/shard_map/pallas_call | solution.py:290
  84.2 1.4 %copy.4 = f32[16,512]{1,0:T(8,128)} copy(f32[16,512]{1,0:T(8,128)} %shard_map.28) | data formatting | bytes 65536

commit v4 on v3

--- a/solution.py
+++ b/solution.py
@@ -98,11 +98,6 @@
             device_id_type=MESH,
         )
 
-    @pl.loop(1, cols)
-    def _(step):
-        _, pc, _ = partner(step)
-        w_copy(c, pc).start()
-
     t_here.wait()
     tdir[pl.ds(pl.multiple_of(me * own, own), own), :] = t_ref[
         :, pl.ds(pl.multiple_of(me * block, 128), block)
@@ -127,6 +122,18 @@
         dh[at, :] = high
         dl[at, :] = low
 
+    left = n - n // 8
+
+    @pl.loop(1, left)
+    def _(step):
+        pr, pc, dest = partner(step)
+        t_copy(me, pr, pc, dest).wait_send()
+
+    @pl.loop(1, cols)
+    def _(step):
+        _, pc, _ = partner(step)
+        w_copy(c, pc).start()
+
     combine(me)
 
     @pl.loop(1, n)
@@ -235,7 +242,7 @@
 
     fr[me] = fbuf[me]
 
-    @pl.loop(1, n)
+    @pl.loop(left, n)
     def _(step):
         pr, pc, dest = partner(step)
         t_copy(me, pr, pc, dest).wait_send()

time: 85.8 us -> 85.7 us (level)
  no operation moved by 1% of the time
where the time goes in v4:
time: 85.7 us; the launch traced here: 85.5 us
  Pallas kernels  84.1 us (98%)
  local copies, waits for them, and re-layouts  1.38 us (2%)
    pallas_call x1, Pallas kernels, in_one_kernel(): pl.pallas_call(functools.partial(cycle_kernel, rows, cols), out_shape=jax...  84.1 us

profile of v4, /device:TPU:0, one launch (start us, length us, event | category | flops | bytes accessed | tf_op | source)
XLA Modules:
  0.0 85.5 jit_solution(17517787721860378738)
XLA Ops:
  0.0 84.1 %shard_map.28 = f32[16,512]{1,0:T(8,128)} custom-call(f32[16,20480]{1,0:T(8,128)} %t_hbm.1, f32[64,5120]{1,0:T(8,128)} %bitcast.1), custom_call_target="tpu_custom_call" | custom-call | flops 1006632960 | bytes 1310720 | tf_op jit(solution)/shard_map/pallas_call | solution.py:297
  84.1 1.4 %copy.4 = f32[16,512]{1,0:T(8,128)} copy(f32[16,512]{1,0:T(8,128)} %shard_map.28) | data formatting | bytes 65536

commit v5 on v4

--- a/solution.py
+++ b/solution.py
@@ -26,10 +26,8 @@
     return high, (x - high.astype(jnp.float32)).astype(jnp.bfloat16)
 
 
-def dot_nt(x, y):
-    return lax.dot_general(
-        x, y, (((1,), (1,)), ((), ())), preferred_element_type=jnp.float32
-    )
+def dot(x, y):
+    return jnp.dot(x, y, preferred_element_type=jnp.float32)
 
 
 def cycle_kernel(
@@ -163,9 +161,11 @@
         )
 
     def multiply(pc):
-        high, low = halves(wr[pc])
-        both = dot_nt(jnp.concatenate([high, low], axis=0), dh[...])
-        pbuf[pc] = both[:chunk] + both[chunk:] + dot_nt(high, dl[...])
+        w = wr[pc]
+        high = w.astype(jnp.bfloat16).astype(jnp.float32)
+        split = jnp.concatenate([high, w - high], axis=0).T.astype(jnp.bfloat16)
+        both = (dot(dh[...], split) + dot(dl[...], split)).T
+        pbuf[pc] = both[:chunk] + both[chunk:]
         for i in range(1, rows):
             r_copy(pc, r, core, (r + i) % rows).start()
 

time: 85.7 us -> 85.8 us (level)
  no operation moved by 1% of the time
where the time goes in v5:
time: 85.8 us; the launch traced here: 85.6 us
  Pallas kernels  84.2 us (98%)
  local copies, waits for them, and re-layouts  1.38 us (2%)
    pallas_call x1, Pallas kernels, in_one_kernel(): pl.pallas_call(functools.partial(cycle_kernel, rows, cols), out_shape=jax...  84.2 us

profile of v5, /device:TPU:0, one launch (start us, length us, event | category | flops | bytes accessed | tf_op | source)
XLA Modules:
  0.0 85.6 jit_solution(504608363481064878)
XLA Ops:
  0.0 84.2 %shard_map.28 = f32[16,512]{1,0:T(8,128)} custom-call(f32[16,20480]{1,0:T(8,128)} %t_hbm.1, f32[64,5120]{1,0:T(8,128)} %bitcast.1), custom_call_target="tpu_custom_call" | custom-call | flops 1006632960 | bytes 1310720 | tf_op jit(solution)/shard_map/pallas_call | solution.py:297
  84.2 1.4 %copy.4 = f32[16,512]{1,0:T(8,128)} copy(f32[16,512]{1,0:T(8,128)} %shard_map.28) | data formatting | bytes 65536

commit v6 on v3

--- a/solution.py
+++ b/solution.py
@@ -83,10 +83,16 @@
             device_id_type=MESH,
         )
 
-    @pl.loop(1, n)
-    def _(step):
+    def t_start(step):
         pr, pc, dest = partner(step)
         t_copy(me, pr, pc, dest).start()
+
+    def t_far():
+        pl.loop(0, n // 2)(lambda i: t_start(2 * i + 1))
+
+    pl.when(core == 0)(t_far)
+    pl.loop(1, n // 2)(lambda i: t_start(2 * i))
+    pl.when(core == 1)(t_far)
 
     def w_copy(sender, dest):
         return pltpu.make_async_remote_copy(
@@ -98,11 +104,15 @@
             device_id_type=MESH,
         )
 
-    @pl.loop(1, cols)
-    def _(step):
-        _, pc, _ = partner(step)
-        w_copy(c, pc).start()
-
+    half = cols // 2
+
+    def w_start(i):
+        far_first = i - 1 + half
+        far_first = far_first - far_first // cols * (cols - 1)
+        w_copy(c, flip(c, far_first + core * (i - far_first), cols)).start()
+
+    w_start(1)
+    w_start(2)
     t_here.wait()
     tdir[pl.ds(pl.multiple_of(me * own, own), own), :] = t_ref[
         :, pl.ds(pl.multiple_of(me * block, 128), block)
@@ -176,9 +186,21 @@
                     total = total + rbuf[pc // 2, sender, side]
         qbuf[pc // 2] = total
 
-    steps = [mask_of(step) for step in range(cols)]
-    ready = {m: max(steps.index(m), steps.index(m + 1)) + 1 for m in range(0, cols, 2)}
-    order = sorted(ready, key=lambda m: ready[m])
+    near = [[m for m in range(1, half) if m % 2 == k] for k in range(2)]
+    far = [[m for m in range(half, cols) if m % 2 == k] for k in range(2)]
+    orders = [
+        [0] + early + first + second[:-1] + late + second[-1:]
+        for early, first, second, late in (
+            (near[1], far[0], far[1], near[0]),
+            (near[0], far[1], far[0], near[1]),
+        )
+    ]
+    codes = [sum(m * cols**i for i, m in enumerate(o)) for o in orders]
+    ready = {
+        m: [max(orders[k].index(m), orders[1 - k].index(m + 1)) + 1 for k in range(2)]
+        for m in range(0, cols, 2)
+    }
+    order = sorted(ready, key=lambda m: max(ready[m]))
 
     def collect_mask(mask):
         pc = flip(c, mask, cols)
@@ -189,18 +211,25 @@
     w_here.wait()
     multiply(c)
 
-    @pl.loop(1, cols)
-    def _(step):
-        _, pc, _ = partner(step)
+    def chunk_step(step, code):
+        pc = flip(c, code % cols, cols)
         w_copy(pc, c).wait_recv()
+        pl.when(step + 2 < cols)(lambda: w_start(step + 2))
         multiply(pc)
         for mask in order:
-            if ready[mask] < cols:
-                pl.when(step == ready[mask])(functools.partial(collect_mask, mask))
+            first, second = ready[mask]
+            pl.when(step == first + core * (second - first))(
+                functools.partial(collect_mask, mask)
+            )
+        return code // cols
+
+    code = codes[0] + core * (codes[1] - codes[0])
+    lax.fori_loop(1, cols, chunk_step, code // cols)
 
     for mask in order:
-        if ready[mask] >= cols:
-            collect_mask(mask)
+        for k in range(2):
+            if ready[mask][k] >= cols:
+                pl.when(core == k)(functools.partial(collect_mask, mask))
 
     full = qbuf[c // 2]
     for mask in order:
@@ -360,7 +389,7 @@
     rows, cols = lax.axis_size("row"), lax.axis_size("col")
     block = width // (rows * cols)
     powers = rows & (rows - 1) == 0 and cols & (cols - 1) == 0
-    whole_tiles = own % 16 == 0 and 128 % own == 0 and block % 128 == 0 and cols > 1
+    whole_tiles = own % 16 == 0 and 128 % own == 0 and block % 128 == 0 and 4 <= cols <= 8
     if OW == 1 and O <= 128 and powers and whole_tiles and block == own * O:
         return in_one_kernel(multiplier, cycle_tiles)
     return in_collectives(multiplier, cycle_tiles)

time: 85.8 us -> 87.6 us (1.021)
  Pallas kernels: 84.2 us -> 86.1 us
    pallas_call x1, Pallas kernels: 84.2 us -> 86.1 us  [in_one_kernel(): pl.pallas_call(functools.partial(cycle_kernel, rows, cols), out_shape=jax...]
where the time goes in v6:
time: 87.6 us; the launch traced here: 87.4 us
  Pallas kernels  86.1 us (98%)
  local copies, waits for them, and re-layouts  1.38 us (2%)
    pallas_call x1, Pallas kernels, in_one_kernel(): pl.pallas_call(functools.partial(cycle_kernel, rows, cols), out_shape=jax...  86.1 us

profile of v6, /device:TPU:0, one launch (start us, length us, event | category | flops | bytes accessed | tf_op | source)
XLA Modules:
  0.0 87.4 jit_solution(1559676262498710774)
XLA Ops:
  0.0 86.1 %shard_map.28 = f32[16,512]{1,0:T(8,128)} custom-call(f32[16,20480]{1,0:T(8,128)} %t_hbm.1, f32[64,5120]{1,0:T(8,128)} %bitcast.1), custom_call_target="tpu_custom_call" | custom-call | flops 1006632960 | bytes 1310720 | tf_op jit(solution)/shard_map/pallas_call | solution.py:319
  86.1 1.4 %copy.4 = f32[16,512]{1,0:T(8,128)} copy(f32[16,512]{1,0:T(8,128)} %shard_map.28) | data formatting | bytes 65536

commit v7 on v4

--- a/solution.py
+++ b/solution.py
@@ -199,11 +199,11 @@
     @pl.loop(1, cols)
     def _(step):
         _, pc, _ = partner(step)
-        w_copy(pc, c).wait_recv()
-        multiply(pc)
         for mask in order:
             if ready[mask] < cols:
                 pl.when(step == ready[mask])(functools.partial(collect_mask, mask))
+        w_copy(pc, c).wait_recv()
+        multiply(pc)
 
     for mask in order:
         if ready[mask] >= cols:

time: 85.7 us -> 91.2 us (1.064)
  Pallas kernels: 84.1 us -> 89.6 us
    pallas_call x1, Pallas kernels: 84.1 us -> 89.6 us  [in_one_kernel(): pl.pallas_call(functools.partial(cycle_kernel, rows, cols), out_shape=jax...]
where the time goes in v7:
time: 91.2 us; the launch traced here: 91 us
  Pallas kernels  89.6 us (98%)
  local copies, waits for them, and re-layouts  1.38 us (2%)
    pallas_call x1, Pallas kernels, in_one_kernel(): pl.pallas_call(functools.partial(cycle_kernel, rows, cols), out_shape=jax...  89.6 us

profile of v7, /device:TPU:0, one launch (start us, length us, event | category | flops | bytes accessed | tf_op | source)
XLA Modules:
  0.0 91.0 jit_solution(5958553612499454952)
XLA Ops:
  0.0 89.6 %shard_map.28 = f32[16,512]{1,0:T(8,128)} custom-call(f32[16,20480]{1,0:T(8,128)} %t_hbm.1, f32[64,5120]{1,0:T(8,128)} %bitcast.1), custom_call_target="tpu_custom_call" | custom-call | flops 1006632960 | bytes 1310720 | tf_op jit(solution)/shard_map/pallas_call | solution.py:297
  89.6 1.4 %copy.4 = f32[16,512]{1,0:T(8,128)} copy(f32[16,512]{1,0:T(8,128)} %shard_map.28) | data formatting | bytes 65536
